TPU v7x, 32 devices: a whole 2x2x4 slice. The times are simulated.
32 devices in a mesh: row: 8 (over z, x), col: 4 (over y, core).
Axes of the slice: x: 2, y: 2, z: 4, core: 2. Of those that a mesh axis runs over, the one named last changes fastest.
Arguments:
- factor: float32 [2, 2048, 2, 1024], P(None, 'row', None, 'col'), may hold values from -5 to 5, as said below
- update: float32 [2, 2048, 512], P(None, 'row', 'col'), may hold values from -1.5 to 1.5
Outputs:
- updated_factor: float32 [2, 2048, 2, 1024], P(None, 'row', None, 'col')
Inputs may be any that keep to these rules, and one draw needn't show every extreme that they name: `factor`: in the first 2048 rows, entries to the right of the diagonal are zero and diagonal entries are positive.
All inputs are finite; a program needn't handle non-finite values.
Results may differ from a plain program's by a relative error of at most 0.0003.
Values sent between devices are 32-bit elements; how exact they have to be, the bound alone decides.
A program may use at most 128 MiB of HBM per device.

v0:
```python
import jax
import jax.numpy as jnp
from jax import lax
from jax.sharding import PartitionSpec as P

PANEL = 1024
TILE = 256
PANELS = 2


def spread(x, axis, root):
    mine = lax.axis_index(axis) == root
    return lax.psum(jnp.where(mine, x, jnp.zeros_like(x)), axis)


def fetch_diag(piece, owner_row):
    return spread(piece, "row", owner_row)


def blocked_cholesky(gram_block):
    order_rows = gram_block.shape[0]
    width = min(TILE, order_rows)
    count_blocks = order_rows // width
    columns = []
    for block_idx in range(count_blocks):
        start = block_idx * width
        current = gram_block[start:, start : start + width]
        for prior_idx in range(block_idx):
            offset = start - prior_idx * width
            prior = columns[prior_idx]
            current = current - jnp.dot(
                prior[offset:],
                prior[offset : offset + width].T,
                precision=lax.Precision.HIGHEST,
                preferred_element_type=jnp.float32,
            )
        diag_factor = jnp.linalg.cholesky(current[:width])
        if block_idx + 1 < count_blocks:
            below = lax.linalg.triangular_solve(
                diag_factor, current[width:], left_side=False, lower=True, transpose_a=True
            )
            columns.append(jnp.concatenate([diag_factor, below], axis=0))
        else:
            columns.append(diag_factor)
    padded = [
        jnp.pad(columns[block_idx], ((block_idx * width, 0), (0, 0)))
        for block_idx in range(count_blocks)
    ]
    return jnp.concatenate(padded, axis=1)


def per_device(factor, update):
    blocks, tile_rows, panels, tile_cols = factor.shape
    rows_here = blocks * tile_rows
    row_devices = lax.axis_size("row")
    row_index = lax.axis_index("row")
    col_index = lax.axis_index("col")
    cycle_rows = row_devices * tile_rows
    factor_width = panels * tile_cols
    own_rows = jnp.concatenate(
        [factor.reshape(rows_here, factor_width), update.reshape(rows_here, update.shape[2])],
        axis=1,
    )
    per_panel = PANEL // TILE
    diag_tiles = PANELS * per_panel
    diagonal_rows = jnp.concatenate(
        [fetch_diag(own_rows[:tile_rows], owner_row) for owner_row in range(diag_tiles)], axis=0
    )

    def select_cols(matrix, panel_idx):
        return jnp.concatenate(
            [matrix[:, : (panel_idx + 1) * tile_cols], matrix[:, factor_width:]], axis=1
        )

    results = []
    later_out = []
    for panel_idx in range(panels):
        row_start = panel_idx * PANEL
        row_end = row_start + PANEL
        panel_rows = select_cols(diagonal_rows[row_start:row_end], panel_idx)
        earlier = [later_out[earlier_idx] for earlier_idx in range(panel_idx)]
        lhs_block = jnp.concatenate([panel_rows] + earlier, axis=1)
        rhs_block = jnp.concatenate([panel_rows] + [-entry for entry in earlier], axis=1)
        gram_block = jnp.dot(
            lhs_block,
            rhs_block.T,
            precision=lax.Precision.HIGHEST,
            preferred_element_type=jnp.float32,
        )
        gram_block = lax.psum(gram_block, "col")
        factor_block = blocked_cholesky(gram_block)
        solved = lax.linalg.triangular_solve(factor_block, rhs_block, left_side=True, lower=True)
        left_rows = jnp.concatenate([select_cols(own_rows, panel_idx)] + results, axis=1)
        if panel_idx + 1 < panels:
            later_block = jnp.concatenate(
                [select_cols(diagonal_rows[row_end:], panel_idx)]
                + [
                    later_out[earlier_idx][row_end - (earlier_idx + 1) * PANEL :]
                    for earlier_idx in range(panel_idx)
                ],
                axis=1,
            )
            left_rows = jnp.concatenate([left_rows, later_block], axis=0)

        def partial_term(begin_row, take_rows, solved=solved, left_rows=left_rows):
            return lax.dot_general(
                solved,
                left_rows,
                (((1,), (1,)), ((), ())),
                precision=lax.Precision.HIGHEST,
                preferred_element_type=jnp.float32,
            )

        shares = lax.psum_scatter(
            partial_term(jnp.int32(0), tile_cols * lax.axis_size("col")),
            "col",
            scatter_dimension=0,
            tiled=True,
        )
        columns_out = shares.T
        results.append(columns_out[:rows_here])
        if panel_idx + 1 < panels:
            later_out.append(columns_out[rows_here:])
    stacked = jnp.stack(results, axis=1)
    local_row = (
        jnp.arange(blocks, dtype=jnp.int32)[:, None] * cycle_rows
        + row_index * tile_rows
        + jnp.arange(tile_rows, dtype=jnp.int32)[None, :]
    ).reshape(rows_here)
    global_col = (
        jnp.arange(panels, dtype=jnp.int32)[:, None] * PANEL
        + col_index * tile_cols
        + jnp.arange(tile_cols, dtype=jnp.int32)[None, :]
    )
    inside_mask = global_col[None, :, :] <= local_row[:, None, None]
    updated = jnp.where(inside_mask, stacked, jnp.zeros_like(stacked))
    return updated.reshape(blocks, tile_rows, panels, tile_cols)


def solution(mesh):
    in_specs = (P(None, "row", None, "col"), P(None, "row", "col"))
    out_specs = P(None, "row", None, "col")
    return jax.shard_map(
        per_device, mesh=mesh, in_specs=in_specs, out_specs=out_specs, check_vma=False
    )
```

profile of v0, /device:TPU:0, one launch (start us, length us, event | category | flops | bytes accessed | tf_op | source)
XLA Modules:
  0.0 1425.8 jit_solution(11416137881681959347)
XLA Ops:
  12.1 189.5 %all-reduce.16.cloned.1.call-done = (f32[256,640]{1,0:T(8,128)}, f32[256,640]{1,0:T(8,128)}, f32[256,640]{1,0:T(8,128)}, f32[256,640]{1,0:T(8,128)}, f32[256,640...) async-done(((f32[256,640]{1,0:T(8,128)}, f32[256,640]{1,0:T(8,128)}, f32[256,640]{1,0:T(8,128)}, f32[256,640]{1,0:T(8,128)}, ...) | async-done | bytes 5242896 | tf_op jit(solution)/shard_map/psum | solution.py:13
  219.1 80.3 %all-reduce.12.cloned.1.call-done = f32[1024,1024]{0,1:T(8,128)} async-done(((f32[1024,1024]{0,1:T(8,128)}), f32[1024,1024]{0,1:T(8,128)}) %all-reduce.12.cloned.1.call-update) | async-done | bytes 4194320 | tf_op jit(solution)/shard_map/psum | solution.py:90
  347.6 20.7 %custom-call.36 = f32[2,128,128]{1,2,0:T(8,128)} custom-call(f32[2,128,128]{2,1,0:T(8,128)S(1)} %get-tuple-element.67), custom_call_target="InvertDiagBlocksLowerTriangular" | custom-call | tf_op jit(solution)/shard_map/triangular_solve/custom-call.0 | solution.py:39
  383.7 13.2 cholesky.416
  415.2 13.3 cholesky.433
  441.3 21.1 %custom-call.38 = f32[2,128,128]{1,2,0:T(8,128)} custom-call(f32[2,128,128]{2,1,0:T(8,128)} %get-tuple-element.68), custom_call_target="InvertDiagBlocksLowerTriangular" | custom-call | tf_op jit(solution)/shard_map/triangular_solve/custom-call.4 | solution.py:39
  478.3 13.2 cholesky.450
  509.9 13.6 cholesky.467
  536.4 21.1 %custom-call.40 = f32[2,128,128]{1,2,0:T(8,128)} custom-call(f32[2,128,128]{2,1,0:T(8,128)} %get-tuple-element.69), custom_call_target="InvertDiagBlocksLowerTriangular" | custom-call | tf_op jit(solution)/shard_map/triangular_solve/custom-call.5 | solution.py:39
  573.3 13.2 cholesky.484
  607.1 13.3 cholesky.501
  634.6 28.0 %while.14 = (s32[]{:T(128)}, f32[1024,1024]{1,0:T(8,128)}, s32[8,2]{0,1:T(2,128)S(1)}, f32[8,128,128]{2,1,0:T(8,128)}, s32[]{:T(128)}) while((s32[]{:T(128)}, f32[1024,1024]{1,0:T(8,128)}, s32[8,2]{0,1:T(2,128)S(1)}, f32[8,128,128]{2,1,0:T(8,128)}, s32[]{:T(128)}) %tuple.215), condition=%wide.while_cond.3, body=%wide.while_body.3.sunk | while | flops 2 | bytes 132205 | solution.py:92
  662.6 80.1 %custom-call.23 = f32[8,128,128]{1,2,0:T(8,128)} custom-call(f32[8,128,128]{2,1,0:T(8,128)} %get-tuple-element.40), custom_call_target="InvertDiagBlocksLowerTriangular" | custom-call | tf_op jit(solution)/shard_map/triangular_solve | solution.py:92
  771.6 58.6 %reduce-scatter.3.cloned.1.call-done = f32[256,1536]{1,0:T(8,128)} async-done(((f32[1024,1536]{1,0:T(8,128)}), f32[256,1536]{1,0:T(8,128)}) %reduce-scatter.3.cloned.1.call-update) | async-done | bytes 1572880 | tf_op jit(solution)/shard_map/reduce_scatter | solution.py:114
  838.1 16.3 %fusion.2 = f32[1024,1024]{0,1:T(8,128)} fusion(f32[1024,640]{1,0:T(8,128)S(1)} %get-tuple-element.287, f32[1024,256]{1,0:T(8,128)} %copy.22, f32[1024,256]{1,0:T(8,128)} %copy.21), kind=kOutput, calls=%fused_computation.49 | convolution fusion | flops 11276124160 | bytes 8912896 | tf_op jit(solution)/shard_map/dot_general | solution.py:84
  856.7 83.3 %all-reduce.14.cloned.1.call-done = f32[1024,1024]{0,1:T(8,128)} async-done(((f32[1024,1024]{0,1:T(8,128)}), f32[1024,1024]{0,1:T(8,128)}) %all-reduce.14.cloned.1.call-update) | async-done | bytes 4194320 | tf_op jit(solution)/shard_map/psum | solution.py:90
  989.8 20.1 %custom-call.43 = f32[2,128,128]{1,2,0:T(8,128)S(1)} custom-call(f32[2,128,128]{2,1,0:T(8,128)S(1)} %get-tuple-element.70), custom_call_target="InvertDiagBlocksLowerTriangular" | custom-call | tf_op jit(solution)/shard_map/triangular_solve/custom-call.0 | solution.py:39
  1071.6 20.5 %custom-call.45 = f32[2,128,128]{1,2,0:T(8,128)S(1)} custom-call(f32[2,128,128]{2,1,0:T(8,128)} %copy-done.51), custom_call_target="InvertDiagBlocksLowerTriangular" | custom-call | tf_op jit(solution)/shard_map/triangular_solve/custom-call.4 | solution.py:39
  1156.0 20.3 %custom-call.47 = f32[2,128,128]{1,2,0:T(8,128)} custom-call(f32[2,128,128]{2,1,0:T(8,128)S(1)} %get-tuple-element.72), custom_call_target="InvertDiagBlocksLowerTriangular" | custom-call | tf_op jit(solution)/shard_map/triangular_solve/custom-call.5 | solution.py:39
  1190.4 13.2 cholesky.620
  1224.3 13.3 cholesky.637
  1251.1 22.4 %while.15 = (s32[]{:T(128)}, f32[1024,1024]{1,0:T(8,128)}, s32[8,2]{0,1:T(2,128)S(1)}, f32[8,128,128]{2,1,0:T(8,128)S(1)}, s32[]{:T(128)}) while((s32[]{:T(128)}, f32[1024,1024]{1,0:T(8,128)}, s32[8,2]{0,1:T(2,128)S(1)}, f32[8,128,128]{2,1,0:T(8,128)S(1)}, s32[]{:T(128)}) %tuple.241), condition=%wide.while_cond.4, body=%wide.while_body.4.sunk | while | flops 2 | bytes 131189 | solution.py:92
  1273.5 79.2 %custom-call.24 = f32[8,128,128]{1,2,0:T(8,128)} custom-call(f32[8,128,128]{2,1,0:T(8,128)S(1)} %get-tuple-element.48), custom_call_target="InvertDiagBlocksLowerTriangular" | custom-call | tf_op jit(solution)/shard_map/triangular_solve | solution.py:92
  1384.0 30.7 %reduce-scatter.5.cloned.1.call-done = f32[256,512]{1,0:T(8,128)} async-done(((f32[1024,512]{1,0:T(8,128)}), f32[256,512]{1,0:T(8,128)}) %reduce-scatter.5.cloned.1.call-update) | async-done | bytes 524304 | tf_op jit(solution)/shard_map/reduce_scatter | solution.py:114
  (435 shorter events, 586.4 us)
Async XLA Ops:
  6.5 195.1 %all-reduce.16.cloned.1.call-start = ((), (), s32[]{:S(2)}) async-start(), calls=%async_computation.6 | async-start | bytes 10485760 | tf_op jit(solution)/shard_map/psum | solution.py:13
  7.8 4.2 copy-start.4
  12.1 287.3 %all-reduce.12.cloned.1.call-start = ((), (), s32[]{:S(2)}) async-start(), calls=%async_computation.2 | async-start | bytes 8388608 | tf_op jit(solution)/shard_map/psum | solution.py:90
  201.6 2.6 copy-start.47
  201.6 2.6 copy-start.46
  215.0 615.2 %reduce-scatter.3.cloned.1.call-start = ((), (), s32[]{:S(2)}) async-start(), calls=%async_computation.3 | async-start | bytes 7864320 | tf_op jit(solution)/shard_map/reduce_scatter | solution.py:114
  347.6 20.7 %copy-start.24 = (f32[256,256]{1,0:T(8,128)}, f32[256,256]{1,0:T(8,128)S(1)}, u32[]{:S(2)}) copy-start(f32[256,256]{1,0:T(8,128)S(1)} %get-tuple-element.683) | copy-start | bytes 786436
  468.4 3.5 copy-start.7
  470.0 2.6 copy-start.9
  563.0 5.0 copy-start.27
  742.7 2.6 copy-start.49
  755.3 3.1 copy-start.14
  755.3 3.1 copy-start.19
  755.3 3.1 copy-start.21
  755.3 3.1 copy-start.22
  771.5 168.5 %all-reduce.14.cloned.1.call-start = ((), (), s32[]{:S(2)}) async-start(), calls=%async_computation.4 | async-start | bytes 8388608 | tf_op jit(solution)/shard_map/psum | solution.py:90
  854.4 560.4 %reduce-scatter.5.cloned.1.call-start = ((), (), s32[]{:S(2)}) async-start(), calls=%async_computation.5 | async-start | bytes 2621440 | tf_op jit(solution)/shard_map/reduce_scatter | solution.py:114
  855.7 129.2 %copy-start.10 = (f32[512,256]{0,1:T(8,128)}, f32[512,256]{0,1:T(8,128)S(1)}, u32[]{:S(2)}) copy-start(f32[512,256]{0,1:T(8,128)S(1)} %slice.496) | copy-start | bytes 1572868
  1098.0 3.4 copy-start.6
  1180.2 4.9 copy-start.28
  1370.8 4.2 copy-start.5
  1370.8 4.2 copy-start.20
  1370.8 4.2 copy-start.23
  1374.9 8.2 copy-start.11
  (34 other events, 34.6 us)
Sparse Core Ops, SparseCore 0:
  12.2 189.3 all-reduce.15
  215.1 84.1 all-reduce.11
  771.6 58.4 reduce-scatter.2
  854.5 85.4 all-reduce.13
  1383.1 31.5 reduce-scatter.4
where the time goes:
time: 1440 us; the launch traced here: 1430 us
  other arithmetic  640 us (44%)
  waiting for transfers between devices  442 us (31%)
  local copies, waits for them, and re-layouts  165 us (11%)
  matrix products  152 us (11%)
  between operations  24.8 us (2%)
    another operation x56, other arithmetic, blocked_cholesky(): diag_factor = jnp.linalg.cholesky(current[:width])  311 us
    psum x1, waiting for transfers between devices, spread(): return lax.psum(jnp.where(mine, x, jnp.zeros_like(x)), axis)  189 us
    another operation x5, other arithmetic, per_device(): lax.linalg.triangular_solve(factor_block, rhs_block, left_side=True, lowe...  167 us
    psum x2, waiting for transfers between devices, per_device(): gram_block = lax.psum(gram_block, 'col')  164 us
    another operation x13, other arithmetic, blocked_cholesky(): lax.linalg.triangular_solve(diag_factor, current[width:], left_side=False...  134 us
    reduce_scatter x2, waiting for transfers between devices, per_device(): lax.psum_scatter(partial_term(jnp.int32(0), tile_cols * lax.axis_size('co...  89.3 us
    another operation x48, local copies, waits for them, and re-layouts  50.3 us
    another operation x49, local copies, waits for them, and re-layouts, blocked_cholesky(): lax.linalg.triangular_solve(diag_factor, current[width:], left_side=False...  42.1 us
  transfers between devices with their start and end apart: 5, of which 5 were waited for; matrix products, arithmetic and copies ran while one was open for 0% of the time, Pallas kernels for 0%

commit v1 on v0

v1 whole, which is shorter than its diff:
```python
import functools

import jax
import jax.numpy as jnp
from jax import lax
from jax.experimental import pallas as pl
from jax.experimental.pallas import tpu as pltpu
from jax.sharding import PartitionSpec as P

PANEL = 1024
PANELS = 2
B=256; H=128; GRP=8
NN=(((1,),(0,)),((),()))
NT=(((1,),(1,)),((),())); TN=(((0,),(0,)),((),()))
def split(x):
    hi=x.astype(jnp.bfloat16); return hi,(x-hi.astype(jnp.float32)).astype(jnp.bfloat16)
def dot3(a,b,dims=NT):
    (ah,al),(bh,bl)=a,b
    d=functools.partial(lax.dot_general,dimension_numbers=dims,preferred_element_type=jnp.float32)
    return d(ah,bh)+(d(ah,bl)+d(al,bh))
def small(a,b,dims=NT):
    return dot3(split(a),split(b),dims)
def factor_half(s_ref, a):
    rows=lax.broadcasted_iota(jnp.int32,(H,H),0); cols=lax.broadcasted_iota(jnp.int32,(H,H),1)
    s_ref[:, :H]=a
    s_ref[:, H:]=(rows==cols).astype(jnp.float32)
    sub=lax.broadcasted_iota(jnp.int32,(GRP,1),0)
    for g in range(H//GRP):
        j=g*GRP
        r=s_ref[j:j+GRP,:]
        cb=[jnp.broadcast_to(r[:,j+b:j+b+1],(GRP,H)) for b in range(GRP)]
        for i in range(GRP):
            rs=lax.rsqrt(cb[i][i:i+1,:])
            m=jnp.where(sub>i,cb[i]*rs,0.0)
            rs2=jnp.concatenate([rs,rs],axis=1); m2=jnp.concatenate([m,m],axis=1)
            u=r[i:i+1,:]*rs2
            r=jnp.where(sub==i,u,r-m2*u)
            for b in range(i+1,GRP):
                cb[b]=cb[b]-m*(cb[b][i:i+1,:]*rs)
        s_ref[j:j+GRP,:]=r
        if j+GRP<H:
            s_ref[j+GRP:,:]=s_ref[j+GRP:,:]-small(r[:,j+GRP:H],r,TN)
    u=jnp.where(rows<=cols,s_ref[:, :H],0.0)
    return u, s_ref[:, H:]

def factor_panel(nrow, ncol, g, ph, plo, inv, s_ref):
    def step(k, _):
        kc = pl.ds(pl.multiple_of(k * B, B), B)
        a = g[k, :, kc]
        u1, v1 = factor_half(s_ref, a[:H, :H])
        l21 = small(a[H:, :H], v1, NT)
        u2, v2 = factor_half(s_ref, a[H:, H:] - small(l21, l21, NT))
        zero = jnp.zeros((H, H), jnp.float32)
        inv[:H, :H] = v1
        inv[:H, H:] = zero
        inv[H:, :H] = -small(v2, small(l21, v1, NN), NN)
        inv[H:, H:] = v2
        g[k, :H, kc] = jnp.concatenate([u1.T, zero], axis=1)
        g[k, H:, kc] = jnp.concatenate([l21, u2.T], axis=1)
        iv = split(inv[...])

        def panel(i, _):
            p = dot3(split(g[i, :, kc]), iv)
            g[i, :, kc] = p
            ph[i], plo[i] = split(p)
            return 0

        lax.fori_loop(k + 1, nrow, panel, 0)

        def colup(j, _):
            jc = pl.ds(pl.multiple_of(j * B, B), B)
            w = (ph[j], plo[j])

            def rowup(i, _):
                g[i, :, jc] = g[i, :, jc] - dot3((ph[i], plo[i]), w)
                return 0

            lax.fori_loop(j, nrow, rowup, 0)
            return 0

        lax.fori_loop(k + 1, ncol, colup, 0)
        return 0

    lax.fori_loop(0, ncol, step, 0)


def panel_kernel(p, ntile, nown, sizes, *refs):
    tc, uc, ncol_dev = sizes
    per = PANEL // B
    first = p * per
    nrow = ntile - first + nown
    if p == 0:
        idx, d_ref, o_ref, out_ref, f_out, xh, xl, g, ph, plo, inv, s_ref = refs
    else:
        idx, d_ref, o_ref, d1_ref, o1_ref, f_in, out_ref, xh, xl, g, ph, plo, inv, s_ref = refs
    width = PANEL + uc * ncol_dev
    for i in range(nrow):
        t = i + first
        src = d_ref if t < ntile else o_ref
        at = (i if p else t) if t < ntile else t - ntile
        for c in range(ncol_dev):
            xh[i, :, c * tc : (c + 1) * tc], xl[i, :, c * tc : (c + 1) * tc] = split(src[at, c, :, :tc])
            lo = PANEL + c * uc
            xh[i, :, lo : lo + uc], xl[i, :, lo : lo + uc] = split(src[at, c, :, tc:])
        if p:
            src = d1_ref if t < ntile else o1_ref
            for c in range(ncol_dev):
                lo = width + c * tc
                xh[i, :, lo : lo + tc], xl[i, :, lo : lo + tc] = split(src[at, c])
            xh[i, :, width + PANEL :], xl[i, :, width + PANEL :] = split(f_in[i])
    full = width + p * PANEL

    def gram_col(j, _):
        jc = pl.ds(pl.multiple_of(j * B, B), B)

        def gram_row(i, _):
            v = dot3((xh[i, :, :full], xl[i, :, :full]), (xh[j, :, :full], xl[j, :, :full]))
            if p:
                v = v - dot3((xh[i, :, full:], xl[i, :, full:]), (xh[j, :, full:], xl[j, :, full:]))
            g[i, :, jc] = v
            return 0

        lax.fori_loop(j, nrow, gram_row, 0)
        return 0

    lax.fori_loop(0, per, gram_col, 0)
    factor_panel(nrow, per, g, ph, plo, inv, s_ref)
    if p == 0:
        f_out[...] = g[per:]
    oc = pl.ds(pl.multiple_of(idx[1] * tc, tc), tc)
    if nown == 1:
        r = idx[0] - first
        t = g[jnp.maximum(r, 0), :, oc]
        keep = idx[1] * (tc // B) <= r
        out_ref[0] = jnp.where(keep, t, 0.0)
        out_ref[1] = g[nrow - 1, :, oc]
    else:
        for e in range(2):
            out_ref[e] = g[nrow - 2 + e, :, oc]


def run_panel(p, idx, ntile, nown, sizes, *arrays):
    tc, uc, nc = sizes
    per = PANEL // B
    nrow = ntile - p * per + nown
    width = PANEL + uc * nc + p * 2 * PANEL
    vm = pl.BlockSpec(memory_space=pltpu.VMEM)
    shape = [jax.ShapeDtypeStruct((2, B, tc), jnp.float32)]
    if p == 0:
        shape.append(jax.ShapeDtypeStruct((nrow - per, B, PANEL), jnp.float32))
    return pl.pallas_call(
        functools.partial(panel_kernel, p, ntile, nown, sizes),
        out_shape=shape,
        in_specs=[pl.BlockSpec(memory_space=pltpu.SMEM)] + [vm] * len(arrays),
        out_specs=[vm] * len(shape),
        scratch_shapes=[
            pltpu.VMEM((nrow, B, width), jnp.bfloat16),
            pltpu.VMEM((nrow, B, width), jnp.bfloat16),
            pltpu.VMEM((nrow, B, PANEL), jnp.float32),
            pltpu.VMEM((nrow, B, B), jnp.bfloat16),
            pltpu.VMEM((nrow, B, B), jnp.bfloat16),
            pltpu.VMEM((B, B), jnp.float32),
            pltpu.VMEM((H, 2 * H), jnp.float32),
        ],
        cost_estimate=pl.CostEstimate(flops=60_000_000_000, bytes_accessed=30_000_000, transcendentals=0),
        compiler_params=pltpu.CompilerParams(vmem_limit_bytes=60 * 2**20),
        name="panel%d" % p,
    )(idx, *arrays)


def per_device(factor, update):
    blocks, tile_rows, panels, tc = factor.shape
    uc = update.shape[2]
    nr, nc = lax.axis_size("row"), lax.axis_size("col")
    r, c = lax.axis_index("row"), lax.axis_index("col")
    ntile = PANELS * PANEL // tile_rows
    whole_rows = nr == ntile
    nown = blocks - 1 if whole_rows else blocks
    sizes = (tc, uc, nc)
    xa = jnp.concatenate([factor[:, :, 0], update], axis=2)
    xb = factor[:, :, 1]

    def diag(x):
        if whole_rows:
            return lax.all_gather(x, ("row", "col")).reshape(ntile, nc, *x.shape)
        tiles = [lax.psum(jnp.where(r == t, x, 0.0), "row") for t in range(ntile)]
        return jnp.moveaxis(lax.all_gather(jnp.stack(tiles), "col"), 0, 1)

    def own(x):
        return jnp.moveaxis(lax.all_gather(x[blocks - nown :], "col"), 0, 1)

    da, oa = diag(xa[0]), own(xa)
    db, ob = diag(xb[0]), own(xb)
    idx = jnp.stack([r, c]).astype(jnp.int32)
    out0, f0 = run_panel(0, idx, ntile, nown, sizes, da, oa)
    (out1,) = run_panel(1, idx, ntile, nown, sizes, da[ntile // 2 :], oa, db[ntile // 2 :], ob, f0)
    out = jnp.stack([out0, out1], axis=2)
    if not whole_rows:
        rows = (
            jnp.arange(blocks)[:, None] * (nr * tile_rows) + r * tile_rows + jnp.arange(tile_rows)
        )
        cols = jnp.arange(panels)[:, None] * PANEL + c * tc + jnp.arange(tc)
        out = jnp.where(cols <= rows[:, :, None, None], out, 0.0)
    return out


def solution(mesh):
    in_specs = (P(None, "row", None, "col"), P(None, "row", "col"))
    out_specs = P(None, "row", None, "col")
    return jax.shard_map(
        per_device, mesh=mesh, in_specs=in_specs, out_specs=out_specs, check_vma=False
    )
```

time: 1440 us -> 432 us (0.30)
  other arithmetic: 640 us -> 3.7 us
  waiting for transfers between devices: 442 us -> 190 us
  Pallas kernels: 0 us -> 207 us
  matrix products: 152 us -> 0 us
  local copies, waits for them, and re-layouts: 165 us -> 17.2 us
    another operation x74 -> x2, other arithmetic: 612 us -> 1.78 us  [the longest x1 1.11 us: per_device(): out = jnp.stack([out0, out1], axis=2)]
    psum x3 -> x0, waiting for transfers between devices: 353 us -> none  [the longest x1 189 us: spread(): return lax.psum(jnp.where(mine, x, jnp.zeros_like(x)), axis)]
    pallas_call x0 -> x2, Pallas kernels: none -> 207 us  [run_panel(): pl.pallas_call(functools.partial(panel_kernel, p, ntile, nown, sizes), ou...]
    all_gather x0 -> x4, waiting for transfers between devices: none -> 190 us  [the longest x2 175 us: diag(): return lax.all_gather(x, ('row', 'col')).reshape(ntile, nc, *x.shape)]
    another operation x122 -> x1, local copies, waits for them, and re-layouts: 112 us -> 1.78 us  [per_device(): out = jnp.stack([out0, out1], axis=2)]
    another operation x64 -> x0, matrix products: 89.4 us -> none  [the longest x30 37.6 us: per_device(): lax.linalg.triangular_solve(factor_block, rhs_block, left_side=True, lowe...]
    reduce_scatter x2 -> x0, waiting for transfers between devices: 89.3 us -> none  [per_device(): lax.psum_scatter(partial_term(jnp.int32(0), tile_cols * lax.axis_size('co...]
    dot_general x16 -> x0, matrix products: 62.8 us -> none  [the longest x2 24.6 us: per_device(): jnp.dot(lhs_block, rhs_block.T, precision=lax.Precision.HIGHEST, preferre...]
  transfers between devices with their start and end apart: 5 -> 4, of which waited for: 5 -> 3; matrix products, arithmetic and copies ran while one was open for 0% -> 4% of each run, Pallas kernels for 0% -> 26%
where the time goes in v1:
time: 432 us; the launch traced here: 431 us
  Pallas kernels  207 us (48%)
  waiting for transfers between devices  190 us (44%)
  local copies, waits for them, and re-layouts  17.2 us (4%)
  between operations  13.2 us (3%)
    pallas_call x2, Pallas kernels, run_panel(): pl.pallas_call(functools.partial(panel_kernel, p, ntile, nown, sizes), ou...  207 us
    all_gather x2, waiting for transfers between devices, diag(): return lax.all_gather(x, ('row', 'col')).reshape(ntile, nc, *x.shape)  175 us
    all_gather x2, waiting for transfers between devices, own(): return jnp.moveaxis(lax.all_gather(x[blocks - nown:], 'col'), 0, 1)  15.2 us
  transfers between devices with their start and end apart: 4, of which 3 were waited for; matrix products, arithmetic and copies ran while one was open for 4% of the time, Pallas kernels for 26%

profile of v1, /device:TPU:0, one launch (start us, length us, event | category | flops | bytes accessed | tf_op | source)
XLA Modules:
  0.0 431.4 jit_solution(1050522024734370956)
XLA Ops:
  6.5 0.0 all-gather.12.cloned.1.call-start
  6.5 1.7 fusion.1
  8.3 0.7 copy.16
  9.0 0.0 all-gather.12.cloned.1.call-update
  9.1 0.0 all-gather.10.cloned.1.call-start
  9.1 1.6 slice.34
  10.7 1.9 pad_maximum_fusion.1
  12.7 0.0 all-gather.10.cloned.1.call-update
  12.7 0.0 all-gather.8.cloned.1.call-start
  12.7 0.7 all-gather.8.cloned.1.call-update
  13.4 0.0 all-gather.14.cloned.1.call-start
  13.5 0.7 copy.17
  14.2 0.0 all-gather.14.cloned.1.call-update
  14.2 0.7 pad_add_fusion.refs_0_
  14.9 75.6 %all-gather.12.cloned.1.call-done = f32[32,256,1,256]{3,1,2,0:T(8,128)} async-done(((f32[1,256,1,256]{3,1,2,0:T(8,128)}), f32[32,256,1,256]{3,1,2,0:T(8,128)}) %all-gather.12.cloned.1.call-update) | async-done | bytes 8388624 | tf_op jit(solution)/shard_map/all_gather | solution.py:185
  90.5 4.6 %slice.48 = f32[16,256,1,256]{3,1,0,2:T(8,128)} slice(f32[32,256,1,256]{3,1,0,2:T(8,128)} %bitcast.17), slice={[16:32], [0:256], [0:1], [0:256]} | slice | bytes 8388608 | tf_op jit(solution)/shard_map/slice | solution.py:196
  95.2 15.2 %all-gather.10.cloned.1.call-done = f32[4,256,384]{2,1,0:T(8,128)} async-done(((f32[1,256,384]{2,1,0:T(8,128)}), f32[4,256,384]{2,1,0:T(8,128)}) %all-gather.10.cloned.1.call-update) | async-done | bytes 1572880 | tf_op jit(solution)/shard_map/all_gather | solution.py:190
  110.4 98.9 %all-gather.8.cloned.1.call-done = f32[32,256,384]{2,1,0:T(8,128)} async-done(((f32[1,256,384]{2,1,0:T(8,128)}), f32[32,256,384]{2,1,0:T(8,128)}) %all-gather.8.cloned.1.call-update) | async-done | bytes 12582928 | tf_op jit(solution)/shard_map/all_gather | solution.py:185
  209.3 110.3 %panel0.1 = (f32[2,256,256]{2,1,0:T(8,128)}, f32[5,256,1024]{2,1,0:T(8,128)}) custom-call(s32[2]{0:T(128)} %pad_add_fusion.refs_0_, f32[8,4,256,384]{3,2,1,0:T(8,128)} %bitcast.15, f32[1,4,256,384]{3,2,1,0:T(8,128)} %bitcast.20), custom_call_target="tpu_custom_call" | custom-call | flops 60000002048 | bytes 30000000 | tf_op jit(solution)/shard_map/panel0/pallas_call | solution.py:151
  319.6 6.0 %slice.47 = f32[16,256,384]{2,1,0:T(8,128)} slice(f32[32,256,384]{2,1,0:T(8,128)} %all-gather.8.cloned.1.call-done), slice={[16:32], [0:256], [0:384]} | slice | bytes 12582912 | tf_op jit(solution)/shard_map/slice | solution.py:196
  325.6 96.4 %panel1.1 = f32[2,256,256]{2,1,0:T(8,128)} custom-call(s32[2]{0:T(128)} %pad_add_fusion.refs_0_, f32[4,4,256,384]{3,2,1,0:T(8,128)} %bitcast.13, f32[1,4,256,384]{3,2,1,0:T(8,128)} %bitcast.21, f32[4,4,256,256]{3,2,1,0:T(8,128)} %bitcast.14, f32[1,4,256,256]{3,2,1,0:T(8,128)} %bitcast.22, f32[5,256,1024]{2,1,0:T(8,128)} %get-tuple-element.8.refs_5_), custom_call_target="tpu_custom_call" | custom-call | flops 60000002048 | bytes 30000000 | tf_op jit(solution)/shard_map/panel1/pallas_call | solution.py:151
  421.9 0.0 copy-done
  421.9 1.1 pad_maximum_fusion
  423.1 1.8 copy.14
  (3 shorter events, 0.0 us)
Async XLA Ops:
  6.5 84.0 %all-gather.12.cloned.1.call-start = ((), (), s32[]{:S(2)}) async-start(), calls=%async_computation.2 | async-start | bytes 8650752 | tf_op jit(solution)/shard_map/all_gather | solution.py:185
  9.1 101.3 %all-gather.10.cloned.1.call-start = ((), (), s32[]{:S(2)}) async-start(), calls=%async_computation.1 | async-start | bytes 1966080 | tf_op jit(solution)/shard_map/all_gather | solution.py:190
  12.7 196.6 %all-gather.8.cloned.1.call-start = ((), (), s32[]{:S(2)}) async-start(), calls=%async_computation | async-start | bytes 12976128 | tf_op jit(solution)/shard_map/all_gather | solution.py:185
  13.4 312.1 %all-gather.14.cloned.1.call-start = ((), (), s32[]{:S(2)}) async-start(), calls=%async_computation.3 | async-start | bytes 1310720 | tf_op jit(solution)/shard_map/all_gather | solution.py:190
  325.6 96.4 %copy-start = (f32[2,256,256]{2,1,0:T(8,128)S(1)}, f32[2,256,256]{2,1,0:T(8,128)}, u32[]{:S(2)}) copy-start(f32[2,256,256]{2,1,0:T(8,128)} %get-tuple-element.7) | copy-start | bytes 1572868
Sparse Core Ops, SparseCore 0:
  10.2 80.2 all-gather.11
  92.1 18.2 all-gather.9
  113.2 95.9 all-gather.7
  210.7 14.9 all-gather.13

commit v2 on v1

--- a/solution.py
+++ b/solution.py
@@ -190,6 +190,7 @@
         return jnp.moveaxis(lax.all_gather(x[blocks - nown :], "col"), 0, 1)
 
     da, oa = diag(xa[0]), own(xa)
+    xb = xb + (da[0, 0, 0, 0] + oa[0, 0, 0, 0]) * 0.0
     db, ob = diag(xb[0]), own(xb)
     idx = jnp.stack([r, c]).astype(jnp.int32)
     out0, f0 = run_panel(0, idx, ntile, nown, sizes, da, oa)

time: 432 us -> 364 us (0.84)
  waiting for transfers between devices: 190 us -> 120 us
    all_gather x2, waiting for transfers between devices: 175 us -> 97.7 us  [diag(): return lax.all_gather(x, ('row', 'col')).reshape(ntile, nc, *x.shape)]
    all_gather x2, waiting for transfers between devices: 15.2 us -> 21.7 us  [own(): return jnp.moveaxis(lax.all_gather(x[blocks - nown:], 'col'), 0, 1)]
  transfers between devices with their start and end apart: 4 -> 4, of which waited for: 3 -> 2; matrix products, arithmetic and copies ran while one was open for 4% -> 3% of each run, Pallas kernels for 26% -> 30%
where the time goes in v2:
time: 364 us; the launch traced here: 363 us
  Pallas kernels  207 us (57%)
  waiting for transfers between devices  120 us (33%)
  local copies, waits for them, and re-layouts  18.2 us (5%)
  between operations  14.4 us (4%)
  other arithmetic  3.67 us (1%)
    pallas_call x2, Pallas kernels, run_panel(): pl.pallas_call(functools.partial(panel_kernel, p, ntile, nown, sizes), ou...  207 us
    all_gather x2, waiting for transfers between devices, diag(): return lax.all_gather(x, ('row', 'col')).reshape(ntile, nc, *x.shape)  97.7 us
    all_gather x2, waiting for transfers between devices, own(): return jnp.moveaxis(lax.all_gather(x[blocks - nown:], 'col'), 0, 1)  21.7 us
  transfers between devices with their start and end apart: 4, of which 2 were waited for; matrix products, arithmetic and copies ran while one was open for 3% of the time, Pallas kernels for 30%

profile of v2, /device:TPU:0, one launch (start us, length us, event | category | flops | bytes accessed | tf_op | source)
XLA Modules:
  0.0 363.3 jit_solution(5765250362775681341)
XLA Ops:
  6.5 0.0 all-gather.10.cloned.1.call-start
  6.5 2.6 fusion.1
  9.2 1.9 pad_maximum_fusion.1
  11.1 0.0 all-gather.10.cloned.1.call-update
  11.1 0.0 all-gather.8.cloned.1.call-start
  11.2 0.7 all-gather.8.cloned.1.call-update
  11.9 0.0 all-gather.12.cloned.1.call-start
  11.9 21.7 %all-gather.10.cloned.1.call-done = f32[4,256,384]{2,1,0:T(8,128)} async-done(((f32[1,256,384]{2,1,0:T(8,128)}), f32[4,256,384]{2,1,0:T(8,128)}) %all-gather.10.cloned.1.call-update) | async-done | bytes 1572880 | tf_op jit(solution)/shard_map/all_gather | solution.py:190
  33.7 1.2 slice.58
  34.9 97.7 %all-gather.8.cloned.1.call-done = f32[32,256,384]{2,1,0:T(8,128)} async-done(((f32[1,256,384]{2,1,0:T(8,128)}), f32[32,256,384]{2,1,0:T(8,128)}) %all-gather.8.cloned.1.call-update) | async-done | bytes 12582928 | tf_op jit(solution)/shard_map/all_gather | solution.py:185
  132.6 1.2 slice.57
  135.1 0.8 fusion.2
  135.9 0.0 all-gather.12.cloned.1.call-update
  136.0 0.0 all-gather.14.cloned.1.call-start
  136.0 0.6 pad_add_fusion.refs_0_
  136.6 0.0 all-gather.14.cloned.1.call-update
  136.6 110.3 %panel0.1 = (f32[2,256,256]{2,1,0:T(8,128)}, f32[5,256,1024]{2,1,0:T(8,128)}) custom-call(s32[2]{0:T(128)} %pad_add_fusion.refs_0_, f32[8,4,256,384]{3,2,1,0:T(8,128)} %bitcast.16, f32[1,4,256,384]{3,2,1,0:T(8,128)} %bitcast.21), custom_call_target="tpu_custom_call" | custom-call | flops 60000002048 | bytes 30000000 | tf_op jit(solution)/shard_map/panel0/pallas_call | solution.py:151
  246.9 6.0 %slice.56 = f32[16,256,384]{2,1,0:T(8,128)} slice(f32[32,256,384]{2,1,0:T(8,128)} %all-gather.8.cloned.1.call-done), slice={[16:32], [0:256], [0:384]} | slice | bytes 12582912 | tf_op jit(solution)/shard_map/slice | solution.py:197
  253.0 0.0 all-gather.12.cloned.1.call-done
  253.0 4.6 %slice.60 = f32[16,256,1,256]{3,1,2,0:T(8,128)} slice(f32[32,256,1,256]{3,1,2,0:T(8,128)} %all-gather.12.cloned.1.call-done), slice={[16:32], [0:256], [0:1], [0:256]} | slice | bytes 8388608 | tf_op jit(solution)/shard_map/slice | solution.py:197
  257.5 96.4 %panel1.1 = f32[2,256,256]{2,1,0:T(8,128)} custom-call(s32[2]{0:T(128)} %pad_add_fusion.refs_0_, f32[4,4,256,384]{3,2,1,0:T(8,128)} %bitcast.13, f32[1,4,256,384]{3,2,1,0:T(8,128)} %bitcast.22, f32[4,4,256,256]{3,2,1,0:T(8,128)} %bitcast.14, f32[1,4,256,256]{3,2,1,0:T(8,128)} %bitcast.23, f32[5,256,1024]{2,1,0:T(8,128)} %get-tuple-element.8.refs_5_), custom_call_target="tpu_custom_call" | custom-call | flops 60000002048 | bytes 30000000 | tf_op jit(solution)/shard_map/panel1/pallas_call | solution.py:151
  353.9 0.0 copy-done
  353.9 1.1 pad_maximum_fusion
  355.0 1.8 copy.8
  (4 shorter events, 0.1 us)
Async XLA Ops:
  6.5 27.1 %all-gather.10.cloned.1.call-start = ((), (), s32[]{:S(2)}) async-start(), calls=%async_computation.1 | async-start | bytes 1966080 | tf_op jit(solution)/shard_map/all_gather | solution.py:190
  11.1 121.4 %all-gather.8.cloned.1.call-start = ((), (), s32[]{:S(2)}) async-start(), calls=%async_computation | async-start | bytes 12976128 | tf_op jit(solution)/shard_map/all_gather | solution.py:185
  11.9 241.1 %all-gather.12.cloned.1.call-start = ((), (), s32[]{:S(2)}) async-start(), calls=%async_computation.2 | async-start | bytes 8650752 | tf_op jit(solution)/shard_map/all_gather | solution.py:185
  136.0 121.6 %all-gather.14.cloned.1.call-start = ((), (), s32[]{:S(2)}) async-start(), calls=%async_computation.3 | async-start | bytes 1310720 | tf_op jit(solution)/shard_map/all_gather | solution.py:190
  257.5 96.4 %copy-start = (f32[2,256,256]{2,1,0:T(8,128)S(1)}, f32[2,256,256]{2,1,0:T(8,128)}, u32[]{:S(2)}) copy-start(f32[2,256,256]{2,1,0:T(8,128)} %get-tuple-element.7) | copy-start | bytes 1572868
Sparse Core Ops, SparseCore 0:
  11.3 22.3 all-gather.9
  36.5 95.9 all-gather.7
  136.1 76.4 all-gather.11
  214.0 15.8 all-gather.13
